TPU v7x, 128 devices: a whole 4x4x4 slice. The times are simulated.
128 devices in a mesh: pose: 16 (over y_hi, z, core), text: 8 (over y_lo, x).
Axes of the slice: x: 4, y: 4 (y_hi: 2, y_lo: 2; y = y_hi * 2 + y_lo), z: 4, core: 2. Of those that a mesh axis runs over, the one named last changes fastest.
Arguments:
- pose_emb: float32 [16384, 768], P(('pose', 'text')), may hold values from -100 to 100
- text_emb: float32 [16384, 768], P(('pose', 'text')), may hold values from -6 to 6
- positive: int32 [16384], P(('pose', 'text')), may hold values from 0 to 16383, each once
Outputs:
- loss: float32 [], replicated
- pose_grad: float32 [16384, 768], P(('pose', 'text'))
- text_grad: float32 [16384, 768], P(('pose', 'text'))
All inputs are finite; a program needn't handle non-finite values.
Results may differ from a plain program's by a relative error of at most 0.0003.
Values sent between devices are 32-bit elements; how exact they have to be, the bound alone decides.
A program may use at most 64 MiB of HBM per device.

v0:
```python
import functools
import math

import jax
import jax.numpy as jnp
from jax import lax
from jax.experimental import pallas as pl
from jax.experimental.pallas import tpu as pltpu
from jax.sharding import PartitionSpec as P

F32 = jnp.float32
BF16 = jnp.bfloat16
U = 128
H = U // 2
LOG2E = math.log2(math.e)


def split(v):
    hi = v.astype(BF16)
    return hi, (v - hi.astype(F32)).astype(BF16)


def dot_nn(a, b):
    return jnp.dot(a, b, preferred_element_type=F32)


ORDER = [(0, 0), (1, 0), (0, 3), (0, 1), (0, 2), (1, 3), (1, 1), (1, 2)]
SLOT = {place: k for k, place in enumerate(ORDER)}
NXT, PRV, PAR = (0, 1), (0, 3), (1, 0)


def kernel(
    scale,
    total,
    pose_ref,
    text_ref,
    pos_ref,
    loss_ref,
    pg_ref,
    tg_ref,
    xf,
    tf,
    xhl,
    xt,
    thl,
    lg,
    sl,
    gp,
    gt,
    rp,
    rt,
    rsib,
    rm,
    rs,
    cm,
    cs,
    rlt,
    idt,
    cv,
    rowst,
    colst,
    rowrec,
    colrec,
    la,
    lb,
    macc,
    ag_send,
    ag_recv,
    sib_send,
    sib_recv,
    group,
    rs_send,
    rs_recv,
    rsib_send,
    rsib_recv,
):
    width = pose_ref.shape[1]
    pi = lax.axis_index("pose")
    ti = lax.axis_index("text")
    yhi, z, core = pi // 8, (pi // 2) % 4, pi % 2
    ylo, x = ti // 4, ti % 4

    def pabs(dy, dx):
        return (ylo + dy) % 2 * 4 + (x + dx) % 4

    def qabs(dy, dz):
        return (yhi + dy) % 2 * 4 + (z + dz) % 4

    def pose_peer(dy, dx):
        return (pi, pabs(dy, dx))

    def text_peer(dy, dz, dc=0):
        return (qabs(dy, dz) * 2 + (core + dc) % 2, (ylo + dy) % 2 * 4 + x)

    pose_peers = [(dy, dx) for dy in range(2) for dx in range(4) if (dy, dx) != (0, 0)]
    text_peers = [
        (dy, dz, dc)
        for dy in range(2)
        for dz in range(4)
        for dc in range(2)
        if (dy, dz, dc) != (0, 0, 0)
    ]

    barrier = pltpu.get_barrier_semaphore()
    near_by = [pose_peer(*d) for d in (NXT, PRV, PAR)]
    near_by += [text_peer(*d) for d in (NXT, PRV, PAR)] + [text_peer(0, 0, 1)]
    for d in near_by:
        pl.semaphore_signal(barrier, inc=1, device_id=d, device_id_type=pl.DeviceIdType.MESH)
    me_p = pabs(0, 0)
    me_q = pi
    xf[me_p] = pose_ref[...]
    tf[me_q] = text_ref[...]
    pl.semaphore_wait(barrier, len(near_by))

    def copy(src, dst, ssem, rsem, dev):
        c = pltpu.make_async_remote_copy(
            src_ref=src,
            dst_ref=dst,
            send_sem=ssem,
            recv_sem=rsem,
            device_id=dev,
            device_id_type=pl.DeviceIdType.MESH,
        )
        c.start()

    def await_recv(dst, rsem):
        pltpu.make_async_copy(dst, dst, rsem).wait()

    def buf(kind, dy, dd, h):
        if kind == 0:
            return xf.at[pabs(dy, dd), pl.ds(h * H, H)]
        return tf.at[qabs(dy, dd) * 2 + core, pl.ds(h * H, H)]

    def peer(kind, dy, dd):
        return pose_peer(dy, dd) if kind == 0 else text_peer(dy, dd, 0)

    def recv_index(place, h):
        return SLOT[place] * 2 + (h if SLOT[place] < 5 else 0)

    def send(kind, src, h, to, arrives):
        b = buf(kind, *src, h)
        copy(b, b, ag_send.at[kind], ag_recv.at[kind, recv_index(arrives, h)], peer(kind, *to))

    def got(kind, place, h):
        await_recv(buf(kind, *place, h), ag_recv.at[kind, SLOT[place] * 2 + h])

    def whole(kind, dy, dd):
        return xf.at[pabs(dy, dd)] if kind == 0 else tf.at[qabs(dy, dd) * 2 + core]

    def got_whole(kind, place):
        await_recv(whole(kind, *place), ag_recv.at[kind, SLOT[place] * 2])

    def share(place):
        b = whole(1, *place)
        copy(b, b, sib_send.at[0], sib_recv.at[SLOT[place]], text_peer(0, 0, 1))

    def got_sib(place):
        await_recv(tf.at[qabs(*place) * 2 + 1 - core], sib_recv.at[SLOT[place]])

    def rows_of(i, n=1):
        return slice(i * U, (i + n) * U)

    def cols_of(j, n=1):
        return slice(j * 2 * U, (j + n) * 2 * U)

    def convert_pose(i):
        v = xf[pabs(*ORDER[i])]
        xhl[0, rows_of(i), :], xhl[1, rows_of(i), :] = split(v)
        xt[0, :, rows_of(i)], xt[1, :, rows_of(i)] = split(v.T)

    def convert_text(j, dc):
        v = tf[qabs(*ORDER[j]) * 2 + (core + dc) % 2]
        rows = rows_of(2 * j + dc)
        thl[0, rows, :], thl[1, rows, :] = split(v)
        sl[0, 0:width, rows], sl[1, 0:width, rows] = split(v.T)

    def stats(i, v, top, total):
        a, b = v[:, 0:U], v[:, U:]
        old = rm[i]
        new = jnp.maximum(jnp.maximum(a, b), old)
        rs[i] = rs[i] * jnp.exp2(old - new) + jnp.exp2(a - new) + jnp.exp2(b - new)
        rm[i] = new
        w = v.reshape(U // 8, 8, 2 * U)
        new = jnp.maximum(top, jnp.max(w, axis=0))
        return new, total * jnp.exp2(top - new) + jnp.sum(jnp.exp2(w - new[None]), axis=0)

    def logits(i, n, j, count=1):
        def body(jj):
            c = pl.ds(pl.multiple_of(jj * 2 * U, 2 * U), 2 * U)
            th, tl = sl[0, 0:width, c], sl[1, 0:width, c]
            top, total = cm[:, c], cs[:, c]
            k = i
            while k < i + n:
                m = min(2, i + n - k)
                r = rows_of(k, m)
                xh, xl = xhl[0, r, :], xhl[1, r, :]
                v = (scale * LOG2E) * (dot_nn(xh, th) + dot_nn(xl, th) + dot_nn(xh, tl))
                lg[r, c] = v
                for q in range(m):
                    top, total = stats(k + q, v[rows_of(q)], top, total)
                k += m
            cm[:, c], cs[:, c] = top, total

        if count == 1:
            body(j)
        else:

            def step(jj, carry):
                body(jj)
                return carry

            lax.fori_loop(j, j + count, step, 0)

    for ref in (rm, cm):
        ref[...] = jnp.full_like(ref, -jnp.inf)
    for ref in (rs, cs):
        ref[...] = jnp.zeros_like(ref)

    for h in range(2):
        for kind in range(2):
            send(kind, (0, 0), h, NXT, (0, 3))
            send(kind, (0, 0), 1 - h, PRV, (0, 1))
            send(kind, (0, 0), h, PAR, (1, 0))
    share((0, 0))
    convert_pose(0)
    convert_text(0, 0)

    for kind in range(2):
        got(kind, (0, 3), 0)
        send(kind, (0, 3), 0, NXT, (0, 2))
        got(kind, (0, 1), 1)
        send(kind, (0, 1), 1, PRV, (0, 2))
    for kind in range(2):
        got(kind, (1, 0), 0)
        send(kind, (1, 0), 0, NXT, (1, 3))
        send(kind, (1, 0), 0, PRV, (1, 1))
    got_sib((0, 0))
    convert_text(0, 1)
    for kind in range(2):
        got(kind, (0, 3), 1)
        got(kind, (0, 1), 0)
    for kind in range(2):
        got(kind, (1, 0), 1)
        send(kind, (1, 0), 1, NXT, (1, 3))
        send(kind, (1, 0), 1, PRV, (1, 1))
    for i in (1, 2, 3):
        share(ORDER[i])
    for i in (1, 2, 3):
        convert_pose(i)
        convert_text(i, 0)
    for j in (1, 2, 3):
        got_sib(ORDER[j])
        convert_text(j, 1)
    logits(0, 4, 0, 4)
    for h in range(2):
        for kind in range(2):
            got(kind, (0, 2), h)
            send(kind, (0, 2), h, PAR, (1, 2))
    share((0, 2))
    convert_pose(4)
    convert_text(4, 0)
    got_sib((0, 2))
    convert_text(4, 1)
    logits(4, 1, 0, 4)
    logits(0, 5, 4)
    for i in (5, 6):
        got_whole(0, ORDER[i])
        convert_pose(i)
    for i in (5, 6):
        got_whole(1, ORDER[i])
        share(ORDER[i])
        convert_text(i, 0)
    logits(5, 2, 0, 5)
    for j in (5, 6):
        got_sib(ORDER[j])
        convert_text(j, 1)
    logits(0, 7, 5, 2)
    for kind in range(2):
        got_whole(kind, (1, 2))
    share((1, 2))
    convert_pose(7)
    convert_text(7, 0)
    logits(7, 1, 0, 7)
    got_sib((1, 2))
    convert_text(7, 1)
    logits(0, 8, 7)

    for i in range(8):
        mt, st = rm[i].T, rs[i].T
        m = jnp.max(mt, axis=0, keepdims=True)
        s = jnp.sum(st * jnp.exp2(mt - m), axis=0, keepdims=True)
        rowst[pl.ds(pabs(*ORDER[i]), 1), :] = m + jnp.log2(s)
    rowst[8:16, :] = jnp.broadcast_to(pos_ref[...].astype(F32), (8, U))
    m = jnp.max(cm[...], axis=0, keepdims=True)
    s = jnp.sum(cs[...] * jnp.exp2(cm[...] - m), axis=0, keepdims=True)
    lse = m + jnp.log2(s)
    for j in range(8):
        for dc in range(2):
            p = qabs(*ORDER[j]) * 2 + (core + dc) % 2
            colst[pl.ds(p, 1), :] = lse[:, rows_of(2 * j + dc)]

    for d in pose_peers:
        copy(rowst, rowrec.at[me_p], group.at[0], group.at[1], pose_peer(*d))
    for d in text_peers:
        copy(colst, colrec.at[me_q], group.at[2], group.at[3], text_peer(*d))
    rowrec[me_p] = rowst[...]
    colrec[me_q] = colst[...]
    await_recv(rowrec.at[0:7], group.at[1])
    await_recv(colrec.at[0:15], group.at[3])

    def lse_of(parts):
        m = parts[0]
        for p in parts[1:]:
            m = jnp.maximum(m, p)
        s = jnp.exp2(parts[0] - m)
        for p in parts[1:]:
            s = s + jnp.exp2(p - m)
        return m + jnp.log2(s)

    rowall, colall = rowrec.at[8], colrec.at[16]
    rowall[0:8] = lse_of([rowrec[k, 0:8, :] for k in range(8)])
    colall[...] = lse_of([colrec[k] for k in range(16)])
    for i in range(8):
        a = pabs(*ORDER[i])
        rlt[i] = jnp.broadcast_to(rowall[pl.ds(a, 1), :] + 1.0, (U, U)).T
        idt[i] = jnp.broadcast_to(rowrec[a, 8:9, :], (U, U)).T

    macc[...] = jnp.zeros_like(macc)
    lane = lax.broadcasted_iota(jnp.int32, (1, U), 1)
    for j, (dy, dz) in enumerate(ORDER):
        for dc in range(2):
            p = qabs(dy, dz) * 2 + (core + dc) % 2
            base = (p * 8 + (ylo + dy) % 2 * 4 + x) * U
            cv[0:1, rows_of(2 * j + dc)] = colall[pl.ds(p, 1), :] + 1.0
            cv[1:2, rows_of(2 * j + dc)] = (base + lane).astype(F32)

    def loop(lo, hi, body):
        def step(k, carry):
            body(k)
            return carry

        if hi > lo:
            lax.fori_loop(lo, hi, step, 0)

    def slope(i2, j):
        acc = None
        for u in range(2):
            rl, ids = rlt[2 * i2 + u], idt[2 * i2 + u]
            r = pl.ds(pl.multiple_of((2 * i2 + u) * U, U), U)
            for dc in range(2):
                c = pl.ds(pl.multiple_of((2 * j + dc) * U, U), U)
                v = lg[r, c]
                hit = ids == cv[1:2, c]
                g = jnp.exp2(v - rl) + jnp.exp2(v - cv[0:1, c])
                t = jnp.where(hit, v, 0.0)
                acc = t if acc is None else acc + t
                hi, lo = split(jnp.where(hit, g - 1.0, g))
                sl[0, r, c] = hi
                sl[1, r, c] = lo
        macc[...] += jnp.sum(acc.reshape(U // 8, 8, U), axis=0)

    reach = {"wide": 8, "tall": 8}

    def slope_for(step, n):
        if step == "Q":
            loop(0, reach["wide"], lambda j: slope(n // 2, j))
            reach["tall"] = n
        else:
            new = min(n, reach["wide"])
            if new < reach["wide"]:
                for j in range(new, reach["wide"]):
                    loop(0, reach["tall"] // 2, lambda i2, j=j: slope(i2, j))
                reach["wide"] = new

    def pose_pair(i):
        r = rows_of(i, 2)

        def body(k):
            c = pl.ds(pl.multiple_of(k * 2 * U, 2 * U), 2 * U)
            sh, sw = sl[0, r, :], sl[1, r, :]
            th = thl[0, :, c]
            g = dot_nn(sh, th) + dot_nn(sh, thl[1, :, c]) + dot_nn(sw, th)
            gp[i, :, c] = g[0:U]
            gp[i + 1, :, c] = g[U:]

        loop(0, width // (2 * U), body)

    def text_pair(j):
        c = cols_of(j)

        def body(k):
            r = pl.ds(pl.multiple_of(k * 2 * U, 2 * U), 2 * U)
            sh, sw = sl[0, :, c], sl[1, :, c]
            xh = xt[0, r, :]
            g = dot_nn(xh, sh) + dot_nn(xh, sw) + dot_nn(xt[1, r, :], sh)
            gt[2 * j, r, :] = g[:, 0:U]
            gt[2 * j + 1, r, :] = g[:, U:]

        loop(0, width // (2 * U), body)
        copy(gt.at[2 * j + 1], rsib.at[j], rsib_send.at[0], rsib_recv.at[j], text_peer(0, 0, 1))

    def g_at(kind, place):
        return gp.at[SLOT[place]] if kind == 0 else gt.at[2 * SLOT[place]]

    def r_at(kind, i):
        return (rp if kind == 0 else rt).at[i]

    def part(ref, h):
        n = ref.shape[0] // 2
        return ref if h is None else ref.at[pl.ds(h * n, n)]

    def rs_index(i, h):
        return i * 2 + (h if i in (0, 3) else 0)

    def rs_send_to(kind, slot, h, to, i):
        copy(
            part(g_at(kind, slot), h),
            part(r_at(kind, i), h),
            rs_send.at[kind],
            rs_recv.at[kind, rs_index(i, h)],
            peer(kind, *to),
        )

    def rs_add(kind, slot, i, h):
        await_recv(part(r_at(kind, i), h), rs_recv.at[kind, rs_index(i, h)])
        dst, src = part(g_at(kind, slot), h), part(r_at(kind, i), h)
        dst[...] += src[...]

    def sib_add(j):
        await_recv(rsib.at[j], rsib_recv.at[j])
        gt[2 * j] += rsib[j]

    def pass_on(step, kind, h):
        if step == "a":
            rs_send_to(kind, (1, 2), h, PAR, 0)
        elif step == "b1":
            rs_send_to(kind, (1, 1), None, NXT, 1)
        elif step == "b2":
            rs_send_to(kind, (1, 3), None, PRV, 2)
        elif step == "c":
            rs_add(kind, (0, 2), 0, h)
            rs_send_to(kind, (0, 2), h, (PRV, NXT)[h], 3)
        elif step == "d":
            rs_add(kind, (1, 0), 1, None)
            rs_add(kind, (1, 0), 2, None)
            rs_send_to(kind, (1, 0), None, PAR, 4)
        else:
            place = (0, 3) if step in ("e0", "f0") else (0, 1)
            if step in ("f0", "f1"):
                rs_add(kind, place, 3, h)
            rs_send_to(kind, place, h, PRV if place == (0, 3) else NXT, 5 if place == (0, 3) else 6)

    def loss_first():
        own = 0.5 * (rowall[pl.ds(me_p, 1), :] + colall[pl.ds(me_q, 1), :])
        first = lax.broadcasted_iota(jnp.int32, (8, U), 0) == 0
        la[me_p] = jnp.where(first, jnp.broadcast_to(own, (8, U)), 0.0) - macc[...]
        b = la.at[me_p]
        for d in pose_peers:
            copy(b, b, group.at[4], group.at[5], pose_peer(*d))

    def loss_second():
        await_recv(la.at[0:7], group.at[5])
        t = la[0]
        for j in range(1, 8):
            t = t + la[j]
        lb[me_q] = t
        b = lb.at[me_q]
        for d in text_peers:
            copy(b, b, group.at[6], group.at[7], text_peer(*d))

    plan = [
        ("Q", 6, 0), ("a", 0, 0), ("a", 0, 1), ("b1", 0, 0), ("T", 7, 0),
        ("T", 6, 0), ("W", 7, 0), ("a", 1, 0), ("a", 1, 1), ("Q", 4, 0), ("c", 0, 0),
        ("b2", 0, 0), ("W", 6, 0), ("b1", 1, 0), ("T", 5, 0),
        ("T", 4, 0), ("c", 0, 1), ("W", 5, 0), ("b2", 1, 0), ("Q", 2, 0),
        ("W", 4, 0), ("c", 1, 0), ("c", 1, 1), ("f0", 0, 0), ("e0", 0, 1), ("e1", 0, 0),
        ("T", 3, 0), ("f1", 0, 1), ("T", 2, 0), ("W", 3, 0), ("e1", 1, 0), ("T", 1, 0),
        ("W", 2, 0), ("e0", 1, 1), ("L1", 0, 0), ("Q", 0, 0), ("L2", 0, 0), ("d", 0, 0),
        ("W", 1, 0), ("d", 1, 0), ("f0", 1, 0), ("f1", 1, 1), ("T", 0, 0),
        ("W", 0, 0),
    ]
    for step, n, h in plan:
        if step == "Q":
            slope_for(step, n)
            pose_pair(n)
        elif step == "T":
            slope_for(step, n)
            text_pair(n)
        elif step == "W":
            sib_add(n)
        elif step == "L1":
            loss_first()
        elif step == "L2":
            loss_second()
        else:
            pass_on(step, n, h)

    for i in (4, 5, 6):
        rs_add(0, (0, 0), i, None)
    pg_ref[...] = scale * gp[0]
    await_recv(lb.at[0:15], group.at[7])
    t = lb[0]
    for j in range(1, 16):
        t = t + lb[j]
    loss_ref[0, 0] = jnp.sum(t) / (total * LOG2E)
    for i in (4, 5, 6):
        rs_add(1, (0, 0), i, None)
    tg_ref[...] = (scale * gt[0]).T

    for kind in range(2):
        await_recv(xf.at[0:7], ag_send.at[kind])
        await_recv(rp, rs_send.at[kind])
    await_recv(xf, sib_send.at[0])
    await_recv(xf, rsib_send.at[0])
    await_recv(rowrec.at[0:7], group.at[0])
    await_recv(colrec.at[0:15], group.at[2])
    await_recv(la.at[0:7], group.at[4])
    await_recv(lb.at[0:15], group.at[6])


def per_device(pose_emb, text_emb, positive):
    rows, width = pose_emb.shape
    total = rows * lax.axis_size("pose") * lax.axis_size("text")
    scale = 2.0 / math.sqrt(width)
    dma = pltpu.SemaphoreType.DMA
    vmem = pltpu.VMEM
    full = pl.BlockSpec(memory_space=pltpu.VMEM)
    loss, pose_grad, text_grad = pl.pallas_call(
        functools.partial(kernel, scale, total),
        out_shape=(
            jax.ShapeDtypeStruct((1, 1), F32),
            jax.ShapeDtypeStruct((rows, width), F32),
            jax.ShapeDtypeStruct((rows, width), F32),
        ),
        in_specs=[full] * 3,
        out_specs=(pl.BlockSpec(memory_space=pltpu.SMEM), full, full),
        scratch_shapes=[
            vmem((8, U, width), F32),
            vmem((16, U, width), F32),
            vmem((2, 8 * U, width), BF16),
            vmem((2, width, 8 * U), BF16),
            vmem((2, 16 * U, width), BF16),
            vmem((8 * U, 16 * U), F32),
            vmem((2, 8 * U, 16 * U), BF16),
            vmem((8, U, width), F32),
            vmem((16, width, U), F32),
            vmem((7, U, width), F32),
            vmem((7, width, U), F32),
            vmem((8, width, U), F32),
            vmem((8, U, U), F32),
            vmem((8, U, U), F32),
            vmem((8, 16 * U), F32),
            vmem((8, 16 * U), F32),
            vmem((8, U, U), F32),
            vmem((8, U, U), F32),
            vmem((8, 16 * U), F32),
            vmem((16, U), F32),
            vmem((16, U), F32),
            vmem((9, 16, U), F32),
            vmem((17, 16, U), F32),
            vmem((8, 8, U), F32),
            vmem((16, 8, U), F32),
            vmem((8, U), F32),
            dma((2,)),
            dma((2, 16)),
            dma((1,)),
            dma((8,)),
            dma((8,)),
            dma((2,)),
            dma((2, 14)),
            dma((1,)),
            dma((8,)),
        ],
        compiler_params=pltpu.CompilerParams(
            collective_id=0, has_side_effects=True, vmem_limit_bytes=64 * 1024 * 1024 - 64 * 1024
        ),
    )(pose_emb, text_emb, positive.reshape(1, rows))
    return (loss.reshape(()), pose_grad, text_grad)


def solution(mesh):
    return jax.shard_map(
        per_device,
        mesh=mesh,
        in_specs=(P(("pose", "text"), None), P(("pose", "text"), None), P(("pose", "text"))),
        out_specs=(P(), P(("pose", "text"), None), P(("pose", "text"), None)),
        check_vma=False,
    )
```

profile of v0, /device:TPU:1, one launch (start us, length us, event | category | flops | bytes accessed | tf_op | source)
XLA Modules:
  0.0 100.7 jit_solution(12104740990803313443)
XLA Ops:
  0.6 95.7 %shard_map.58 = (f32[1,1]{1,0:T(1,128)}, f32[128,768]{1,0:T(8,128)}, f32[128,768]{1,0:T(8,128)}) custom-call(f32[128,768]{1,0:T(8,128)} %pose_ref.1, f32[128,768]{1,0:T(8,128)} %text_ref.1, s32[1,128]{1,0:T(1,128)} %bitcast.2), custom_call_target="tpu_custom_call" | custom-call | tf_op jit(solution)/shard_map/pallas_call | solution.py:528
  97.0 0.0 copy-start
  97.0 1.8 %copy.10 = f32[128,768]{1,0:T(8,128)} copy(f32[128,768]{1,0:T(8,128)} %get-tuple-element.13) | data formatting | bytes 786432
  98.8 0.0 copy-done
  98.8 0.7 copy.11
Async XLA Ops:
  97.0 1.8 %copy-start = (f32[128,768]{1,0:T(8,128)S(1)}, f32[128,768]{1,0:T(8,128)}, u32[]{:S(2)}) copy-start(f32[128,768]{1,0:T(8,128)} %get-tuple-element.14) | copy-start | bytes 1179652
where the time goes:
time: 101 us
  Pallas kernels  95.7 us (95%)
  local copies, waits for them, and re-layouts  2.57 us (3%)
  between operations  2.41 us (2%)
    pallas_call x1, Pallas kernels, per_device(): pl.pallas_call(functools.partial(kernel, scale, total), out_shape=(jax.Sh...  95.7 us
    unnamed x4, local copies, waits for them, and re-layouts  2.57 us

commit v1 on v0

--- a/solution.py
+++ b/solution.py
@@ -22,6 +22,12 @@
 
 def dot_nn(a, b):
     return jnp.dot(a, b, preferred_element_type=F32)
+
+
+def dot3(ah, al, bh, bl):
+    n = ah.shape[0]
+    both = dot_nn(jnp.concatenate([ah, al], axis=0), bh)
+    return both[:n] + (both[n:] + dot_nn(ah, bl))
 
 
 ORDER = [(0, 0), (1, 0), (0, 3), (0, 1), (0, 2), (1, 3), (1, 1), (1, 2)]
@@ -194,7 +200,7 @@
                 m = min(2, i + n - k)
                 r = rows_of(k, m)
                 xh, xl = xhl[0, r, :], xhl[1, r, :]
-                v = (scale * LOG2E) * (dot_nn(xh, th) + dot_nn(xl, th) + dot_nn(xh, tl))
+                v = (scale * LOG2E) * dot3(xh, xl, th, tl)
                 lg[r, c] = v
                 for q in range(m):
                     top, total = stats(k + q, v[rows_of(q)], top, total)
@@ -379,7 +385,7 @@
             c = pl.ds(pl.multiple_of(k * 2 * U, 2 * U), 2 * U)
             sh, sw = sl[0, r, :], sl[1, r, :]
             th = thl[0, :, c]
-            g = dot_nn(sh, th) + dot_nn(sh, thl[1, :, c]) + dot_nn(sw, th)
+            g = dot3(sh, sw, th, thl[1, :, c])
             gp[i, :, c] = g[0:U]
             gp[i + 1, :, c] = g[U:]
 
@@ -392,7 +398,7 @@
             r = pl.ds(pl.multiple_of(k * 2 * U, 2 * U), 2 * U)
             sh, sw = sl[0, :, c], sl[1, :, c]
             xh = xt[0, r, :]
-            g = dot_nn(xh, sh) + dot_nn(xh, sw) + dot_nn(xt[1, r, :], sh)
+            g = dot3(xh, xt[1, r, :], sh, sw)
             gt[2 * j, r, :] = g[:, 0:U]
             gt[2 * j + 1, r, :] = g[:, U:]
 
@@ -475,9 +481,9 @@
         ("T", 4, 0), ("c", 0, 1), ("W", 5, 0), ("b2", 1, 0), ("Q", 2, 0),
         ("W", 4, 0), ("c", 1, 0), ("c", 1, 1), ("f0", 0, 0), ("e0", 0, 1), ("e1", 0, 0),
         ("T", 3, 0), ("f1", 0, 1), ("T", 2, 0), ("W", 3, 0), ("e1", 1, 0), ("T", 1, 0),
-        ("W", 2, 0), ("e0", 1, 1), ("L1", 0, 0), ("Q", 0, 0), ("L2", 0, 0), ("d", 0, 0),
+        ("W", 2, 0), ("e0", 1, 1), ("Q", 0, 0), ("L1", 0, 0), ("d", 0, 0),
         ("W", 1, 0), ("d", 1, 0), ("f0", 1, 0), ("f1", 1, 1), ("T", 0, 0),
-        ("W", 0, 0),
+        ("W", 0, 0), ("L2", 0, 0),
     ]
     for step, n, h in plan:
         if step == "Q":

time: 101 us -> 99.4 us (0.984)
  Pallas kernels: 95.7 us -> 94.3 us
    pallas_call x1, Pallas kernels: 95.7 us -> 94.3 us  [per_device(): pl.pallas_call(functools.partial(kernel, scale, total), out_shape=(jax.Sh...]
where the time goes in v1:
time: 99.4 us; the launch traced here: 99.3 us
  Pallas kernels  94.3 us (95%)
  local copies, waits for them, and re-layouts  2.57 us (3%)
  between operations  2.41 us (2%)
    pallas_call x1, Pallas kernels, per_device(): pl.pallas_call(functools.partial(kernel, scale, total), out_shape=(jax.Sh...  94.3 us
    unnamed x4, local copies, waits for them, and re-layouts  2.57 us

profile of v1, /device:TPU:1, one launch (start us, length us, event | category | flops | bytes accessed | tf_op | source)
XLA Modules:
  0.0 99.3 jit_solution(6769730600169936520)
XLA Ops:
  0.6 94.3 %shard_map.58 = (f32[1,1]{1,0:T(1,128)}, f32[128,768]{1,0:T(8,128)}, f32[128,768]{1,0:T(8,128)}) custom-call(f32[128,768]{1,0:T(8,128)} %pose_ref.1, f32[128,768]{1,0:T(8,128)} %text_ref.1, s32[1,128]{1,0:T(1,128)} %bitcast.2), custom_call_target="tpu_custom_call" | custom-call | tf_op jit(solution)/shard_map/pallas_call | solution.py:534
  95.6 0.0 copy-start
  95.6 1.8 %copy.10 = f32[128,768]{1,0:T(8,128)} copy(f32[128,768]{1,0:T(8,128)} %get-tuple-element.13) | data formatting | bytes 786432
  97.4 0.0 copy-done
  97.4 0.7 copy.11
Async XLA Ops:
  95.6 1.8 %copy-start = (f32[128,768]{1,0:T(8,128)S(1)}, f32[128,768]{1,0:T(8,128)}, u32[]{:S(2)}) copy-start(f32[128,768]{1,0:T(8,128)} %get-tuple-element.14) | copy-start | bytes 1179652

commit v2 on v1

--- a/solution.py
+++ b/solution.py
@@ -30,7 +30,7 @@
     return both[:n] + (both[n:] + dot_nn(ah, bl))
 
 
-ORDER = [(0, 0), (1, 0), (0, 3), (0, 1), (0, 2), (1, 3), (1, 1), (1, 2)]
+ORDER = [(0, 0), (0, 3), (0, 1), (1, 0), (0, 2), (1, 3), (1, 1), (1, 2)]
 SLOT = {place: k for k, place in enumerate(ORDER)}
 NXT, PRV, PAR = (0, 1), (0, 3), (1, 0)
 
@@ -257,12 +257,13 @@
     for j in (1, 2, 3):
         got_sib(ORDER[j])
         convert_text(j, 1)
-    logits(0, 4, 0, 4)
+    logits(0, 4, 0, 2)
     for h in range(2):
         for kind in range(2):
             got(kind, (0, 2), h)
             send(kind, (0, 2), h, PAR, (1, 2))
     share((0, 2))
+    logits(0, 4, 2, 2)
     convert_pose(4)
     convert_text(4, 0)
     got_sib((0, 2))
@@ -368,9 +369,11 @@
     reach = {"wide": 8, "tall": 8}
 
     def slope_for(step, n):
-        if step == "Q":
-            loop(0, reach["wide"], lambda j: slope(n // 2, j))
-            reach["tall"] = n
+        if step != "T":
+            pair = {6: 3, 4: 2, 3: 1, 1: 0}.get(n)
+            if pair is not None:
+                loop(0, reach["wide"], lambda j: slope(pair, j))
+                reach["tall"] = 2 * pair
         else:
             new = min(n, reach["wide"])
             if new < reach["wide"]:
@@ -378,16 +381,16 @@
                     loop(0, reach["tall"] // 2, lambda i2, j=j: slope(i2, j))
                 reach["wide"] = new
 
-    def pose_pair(i):
-        r = rows_of(i, 2)
+    def pose_rows(i, n):
+        r = rows_of(i, n)
 
         def body(k):
             c = pl.ds(pl.multiple_of(k * 2 * U, 2 * U), 2 * U)
             sh, sw = sl[0, r, :], sl[1, r, :]
             th = thl[0, :, c]
             g = dot3(sh, sw, th, thl[1, :, c])
-            gp[i, :, c] = g[0:U]
-            gp[i + 1, :, c] = g[U:]
+            for u in range(n):
+                gp[i + u, :, c] = g[rows_of(u)]
 
         loop(0, width // (2 * U), body)
 
@@ -475,20 +478,19 @@
             copy(b, b, group.at[6], group.at[7], text_peer(*d))
 
     plan = [
-        ("Q", 6, 0), ("a", 0, 0), ("a", 0, 1), ("b1", 0, 0), ("T", 7, 0),
-        ("T", 6, 0), ("W", 7, 0), ("a", 1, 0), ("a", 1, 1), ("Q", 4, 0), ("c", 0, 0),
-        ("b2", 0, 0), ("W", 6, 0), ("b1", 1, 0), ("T", 5, 0),
-        ("T", 4, 0), ("c", 0, 1), ("W", 5, 0), ("b2", 1, 0), ("Q", 2, 0),
-        ("W", 4, 0), ("c", 1, 0), ("c", 1, 1), ("f0", 0, 0), ("e0", 0, 1), ("e1", 0, 0),
-        ("T", 3, 0), ("f1", 0, 1), ("T", 2, 0), ("W", 3, 0), ("e1", 1, 0), ("T", 1, 0),
-        ("W", 2, 0), ("e0", 1, 1), ("Q", 0, 0), ("L1", 0, 0), ("d", 0, 0),
-        ("W", 1, 0), ("d", 1, 0), ("f0", 1, 0), ("f1", 1, 1), ("T", 0, 0),
-        ("W", 0, 0), ("L2", 0, 0),
+        ("T", 7, 0), ("Q", 6, 0), ("a", 0, 0), ("a", 0, 1), ("W", 7, 0), ("a", 1, 0),
+        ("a", 1, 1), ("b1", 0, 0), ("Q", 4, 0), ("b2", 0, 0), ("T", 6, 0), ("c", 0, 0),
+        ("T", 5, 0), ("W", 6, 0), ("b1", 1, 0), ("T", 4, 0), ("c", 0, 1), ("W", 5, 0),
+        ("b2", 1, 0), ("T", 3, 0), ("W", 4, 0), ("c", 1, 0), ("c", 1, 1), ("T", 2, 0),
+        ("T", 1, 0), ("W", 2, 0), ("e1", 1, 0), ("P", 3, 0), ("d", 0, 0), ("W", 1, 0),
+        ("e0", 1, 1), ("Q", 1, 0), ("L1", 0, 0), ("W", 3, 0), ("d", 1, 0), ("f0", 0, 0),
+        ("f1", 0, 1), ("f1", 1, 1), ("e0", 0, 1), ("e1", 0, 0), ("P", 0, 0), ("f0", 1, 0),
+        ("T", 0, 0), ("W", 0, 0), ("L2", 0, 0),
     ]
     for step, n, h in plan:
-        if step == "Q":
+        if step in ("Q", "P"):
             slope_for(step, n)
-            pose_pair(n)
+            pose_rows(n, 2 if step == "Q" else 1)
         elif step == "T":
             slope_for(step, n)
             text_pair(n)

time: 99.4 us -> 97.5 us (0.981)
  Pallas kernels: 94.3 us -> 92.3 us
    pallas_call x1, Pallas kernels: 94.3 us -> 92.3 us  [per_device(): pl.pallas_call(functools.partial(kernel, scale, total), out_shape=(jax.Sh...]
where the time goes in v2:
time: 97.5 us; the launch traced here: 97.3 us
  Pallas kernels  92.3 us (95%)
  local copies, waits for them, and re-layouts  2.57 us (3%)
  between operations  2.41 us (2%)
    pallas_call x1, Pallas kernels, per_device(): pl.pallas_call(functools.partial(kernel, scale, total), out_shape=(jax.Sh...  92.3 us
    unnamed x4, local copies, waits for them, and re-layouts  2.57 us

profile of v2, /device:TPU:1, one launch (start us, length us, event | category | flops | bytes accessed | tf_op | source)
XLA Modules:
  0.0 97.3 jit_solution(3340411392925378924)
XLA Ops:
  0.6 92.3 %shard_map.58 = (f32[1,1]{1,0:T(1,128)}, f32[128,768]{1,0:T(8,128)}, f32[128,768]{1,0:T(8,128)}) custom-call(f32[128,768]{1,0:T(8,128)} %pose_ref.1, f32[128,768]{1,0:T(8,128)} %text_ref.1, s32[1,128]{1,0:T(1,128)} %bitcast.2), custom_call_target="tpu_custom_call" | custom-call | tf_op jit(solution)/shard_map/pallas_call | solution.py:536
  93.6 0.0 copy-start
  93.6 1.8 %copy.10 = f32[128,768]{1,0:T(8,128)} copy(f32[128,768]{1,0:T(8,128)} %get-tuple-element.13) | data formatting | bytes 786432
  95.4 0.0 copy-done
  95.4 0.7 copy.11
Async XLA Ops:
  93.6 1.8 %copy-start = (f32[128,768]{1,0:T(8,128)S(1)}, f32[128,768]{1,0:T(8,128)}, u32[]{:S(2)}) copy-start(f32[128,768]{1,0:T(8,128)} %get-tuple-element.14) | copy-start | bytes 1179652

commit v3 on v2

--- a/solution.py
+++ b/solution.py
@@ -207,15 +207,19 @@
                 k += m
             cm[:, c], cs[:, c] = top, total
 
+        wide = 2 if n <= 2 and count > 1 else 1
+
+        def step(k, carry):
+            for u in range(wide):
+                body(j + k * wide + u)
+            return carry
+
         if count == 1:
             body(j)
         else:
-
-            def step(jj, carry):
-                body(jj)
-                return carry
-
-            lax.fori_loop(j, j + count, step, 0)
+            lax.fori_loop(0, count // wide, step, 0)
+            if count % wide:
+                body(j + count - 1)
 
     for ref in (rm, cm):
         ref[...] = jnp.full_like(ref, -jnp.inf)
@@ -505,7 +509,7 @@
 
     for i in (4, 5, 6):
         rs_add(0, (0, 0), i, None)
-    pg_ref[...] = scale * gp[0]
+    pg_ref[...] = gp[0]
     await_recv(lb.at[0:15], group.at[7])
     t = lb[0]
     for j in range(1, 16):
@@ -513,7 +517,7 @@
     loss_ref[0, 0] = jnp.sum(t) / (total * LOG2E)
     for i in (4, 5, 6):
         rs_add(1, (0, 0), i, None)
-    tg_ref[...] = (scale * gt[0]).T
+    tg_ref[...] = gt[0].T
 
     for kind in range(2):
         await_recv(xf.at[0:7], ag_send.at[kind])
@@ -583,7 +587,7 @@
             collective_id=0, has_side_effects=True, vmem_limit_bytes=64 * 1024 * 1024 - 64 * 1024
         ),
     )(pose_emb, text_emb, positive.reshape(1, rows))
-    return (loss.reshape(()), pose_grad, text_grad)
+    return (loss.reshape(()), scale * pose_grad, scale * text_grad)
 
 
 def solution(mesh):

time: 97.5 us -> 96.3 us (0.988)
  local copies, waits for them, and re-layouts: 2.57 us -> 0 us
  other arithmetic: 0 us -> 2.06 us
    unnamed x4 -> x0, local copies, waits for them, and re-layouts: 2.57 us -> none
    mul x0 -> x1, other arithmetic: none -> 2.06 us  [per_device(): return (loss.reshape(()), scale * pose_grad, scale * text_grad)]
where the time goes in v3:
time: 96.3 us; the launch traced here: 96.2 us
  Pallas kernels  91.7 us (95%)
  between operations  2.4 us (2%)
  other arithmetic  2.06 us (2%)
    pallas_call x1, Pallas kernels, per_device(): pl.pallas_call(functools.partial(kernel, scale, total), out_shape=(jax.Sh...  91.7 us
    mul x1, other arithmetic, per_device(): return (loss.reshape(()), scale * pose_grad, scale * text_grad)  2.06 us

profile of v3, /device:TPU:1, one launch (start us, length us, event | category | flops | bytes accessed | tf_op | source)
XLA Modules:
  0.0 96.2 jit_solution(15976235123291482497)
XLA Ops:
  0.6 91.7 %shard_map.58 = (f32[1,1]{1,0:T(1,128)}, f32[128,768]{1,0:T(8,128)}, f32[128,768]{1,0:T(8,128)}) custom-call(f32[128,768]{1,0:T(8,128)} %pose_ref.1, f32[128,768]{1,0:T(8,128)} %text_ref.1, s32[1,128]{1,0:T(1,128)} %bitcast.2), custom_call_target="tpu_custom_call" | custom-call | tf_op jit(solution)/shard_map/pallas_call | solution.py:540
  92.3 2.1 %broadcast_multiply_fusion = (f32[128,768]{1,0:T(8,128)}, f32[128,768]{1,0:T(8,128)}) fusion(f32[128,768]{1,0:T(8,128)} %get-tuple-element.8, f32[128,768]{1,0:T(8,128)} %get-tuple-element.7), kind=kLoop, calls=%fused_computation | loop fusion | flops 196608 | bytes 1572864 | tf_op jit(solution)/shard_map/mul | solution.py:590
